TPU v7x, 32 devices: a whole 2x2x4 slice. The times are simulated.
32 devices in a mesh: groups: 2 (over y), bins: 4 (over z), blk: 4 (over x, core).
Axes of the slice: x: 2, y: 2, z: 4, core: 2. Of those that a mesh axis runs over, the one named last changes fastest.
Arguments:
- tokens: bfloat16 [32768, 1024], P(('groups', 'bins', 'blk')), parts along dimension 0, may hold values from -6 to 6
- enc_gain: float32 [1024], replicated, may hold values from 0.25 to 1.75
- enc_weight: bfloat16 [1024, 1024], replicated, may hold values from -0.1875 to 0.1875
- lengths: int32 [32, 256], P(('groups', 'bins', 'blk')), parts along dimension 0, may hold values from 1 to 16, 1024 in all within a row
- membership: int32 [8192, 1], P(('groups', 'bins', 'blk')), parts along dimension 0, may hold values from 0 to 3; in each aligned block of 256 rows (0 to 255, 256 to 511, ...) at most 80 rows name the same one
- target_keys: int32 [8192], P(('groups', 'bins', 'blk')), parts along dimension 0, may hold values from 0 to 4095, as said below
- key_weight: bfloat16 [1024, 1024], replicated, may hold values from -0.1875 to 0.1875
- value_weight: bfloat16 [1024, 1024], replicated, may hold values from -0.1875 to 0.1875
- query_weight: bfloat16 [1024, 1024], replicated, may hold values from -0.1875 to 0.1875
- out_weight: bfloat16 [1024, 1024], replicated, may hold values from -0.1875 to 0.1875
- inducing: bfloat16 [32, 1024], replicated, may hold values from -256 to 256
- score_vector: float32 [1024], replicated, may hold values from -0.1875 to 0.1875
Outputs:
- row_grads: bfloat16 [8192, 1024], P(('groups', 'bins', 'blk')), parts along dimension 0
- slate_loss: float32 [8], P(('groups', 'bins')), parts along dimension 0
There are 2 independent parts, one for each index of `groups`. A program takes and returns all parts, laid end to end along the dimension named above; an argument that names none is the same for every part. Nothing has to cross between parts.
Inputs may be any that keep to these rules, and one draw needn't show every extreme that they name: `membership`: within the candidates of one bin, no slate holds more than 80; some slate holds exactly 80 of some bin's candidates; every slate holds some candidate. Each bin's lengths sum to 1024. `target_keys`: each key appears once.
All inputs are finite; a program needn't handle non-finite values.
Results may differ from a plain program's by a relative error of at most 0.017.
The roundings to bfloat16 on the way count: a program that leaves them out, or rounds other values in their place, can miss the bound.
Values may be sent and summed in bfloat16 or wider, within the bound.
A program may use at most 64 MiB of HBM per device.

v0:
```python
import jax
import jax.numpy as jnp
from jax import lax
from jax.sharding import PartitionSpec as P

HEADS = 16
HD = 64
INDUCE = 32


def fold_induced(carry, keys_piece, values_piece, valid_piece, inducing):
    run_max, run_sum, run_acc = carry
    count = keys_piece.shape[0]
    head_keys = keys_piece.reshape(count, HEADS, HD)
    head_vals = values_piece.reshape(count, HEADS, HD).astype(jnp.float32)
    queries = inducing.reshape(INDUCE, HEADS, HD)
    scores = jnp.einsum(
        "ihd,nhd->hin", queries, head_keys, preferred_element_type=jnp.float32
    ) / jnp.sqrt(jnp.float32(HD))
    usable = valid_piece > 0
    scores = jnp.where(usable[None, None, :], scores, -1e30)
    new_max = jnp.maximum(run_max, jnp.max(scores, axis=-1))
    probs = jnp.where(usable[None, None, :], jnp.exp(scores - new_max[..., None]), 0.0)
    new_sum = jnp.sum(probs, axis=-1)
    new_acc = jnp.einsum("hin,nhd->hid", probs, head_vals)
    return (new_max, new_sum, new_acc)


def doc_scores(rows_f, induced, query_weight, out_weight, score_vector):
    count = rows_f.shape[0]
    rows_b = rows_f.astype(jnp.bfloat16)
    quer = jnp.dot(rows_b, query_weight, preferred_element_type=jnp.float32).astype(jnp.bfloat16)
    quer = quer.reshape(count, HEADS, HD)
    head_ind = induced.reshape(INDUCE, HEADS, HD)
    scores = jnp.einsum(
        "nhd,jhd->nhj", quer, head_ind, preferred_element_type=jnp.float32
    ) / jnp.sqrt(jnp.float32(HD))
    weights = jax.nn.softmax(scores, axis=-1).astype(jnp.bfloat16)
    mixed = jnp.einsum("nhj,jhd->nhd", weights, head_ind, preferred_element_type=jnp.float32)
    mixed = mixed.reshape(count, HEADS * HD).astype(jnp.bfloat16)
    full = rows_f + jnp.dot(mixed, out_weight, preferred_element_type=jnp.float32)
    return jnp.sum(full * score_vector, axis=-1)


def local(
    tokens,
    enc_gain,
    enc_weight,
    lengths,
    membership,
    target_keys,
    key_weight,
    value_weight,
    query_weight,
    out_weight,
    inducing,
    score_vector,
):
    tok_count = tokens.shape[0]
    xf = tokens.astype(jnp.float32)
    meansq = jnp.mean(xf * xf, axis=-1, keepdims=True)
    normed = (xf * lax.rsqrt(meansq + 1e-06) * enc_gain).astype(jnp.bfloat16)
    enc_tok = (xf + jnp.dot(normed, enc_weight, preferred_element_type=jnp.float32)).astype(
        jnp.bfloat16
    )
    lens = lengths[0]
    cand = lens.shape[0]
    ends = jnp.cumsum(lens)
    starts = ends - lens
    position = jnp.arange(tok_count, dtype=jnp.int32)
    member_tok = (position[None, :] >= starts[:, None]) & (position[None, :] < ends[:, None])
    pooled = jnp.dot(member_tok.astype(jnp.bfloat16), enc_tok, preferred_element_type=jnp.float32)
    encoded = (pooled / lens[:, None].astype(jnp.float32)).astype(jnp.bfloat16)
    nbins = lax.axis_size("bins")
    slots = max(2, 5 * cand // (4 * nbins))
    total_slots = nbins * slots
    dest = membership[:, 0]
    order = jnp.arange(cand, dtype=jnp.int32)
    same_dest = (dest[:, None] == dest[None, :]) & (order[:, None] > order[None, :])
    rank = jnp.sum(same_dest.astype(jnp.int32), axis=1)
    slot_of = dest * slots + rank
    placed = jnp.arange(total_slots, dtype=jnp.int32)[:, None] == slot_of[None, :]
    placed_b = placed.astype(jnp.bfloat16)
    send_rows = jnp.dot(placed_b, encoded, preferred_element_type=jnp.float32).astype(jnp.bfloat16)
    send_tags = jnp.sum(jnp.where(placed, target_keys[None, :] + 1, 0), axis=1)
    width = encoded.shape[1]
    slate_rows = lax.all_to_all(
        send_rows.reshape(nbins, slots, width), "bins", split_axis=0, concat_axis=0, tiled=True
    ).reshape(total_slots, width)
    tags = lax.all_to_all(
        send_tags.reshape(nbins, slots), "bins", split_axis=0, concat_axis=0, tiled=True
    ).reshape(total_slots)
    valid = tags > 0
    valid_b = valid.astype(jnp.bfloat16)
    keys = jnp.dot(slate_rows, key_weight, preferred_element_type=jnp.float32).astype(jnp.bfloat16)
    values = jnp.dot(slate_rows, value_weight, preferred_element_type=jnp.float32).astype(
        jnp.bfloat16
    )
    start_state = (
        jnp.full((HEADS, INDUCE), -1e30, jnp.float32),
        jnp.zeros((HEADS, INDUCE), jnp.float32),
        jnp.zeros((HEADS, INDUCE, HD), jnp.float32),
    )
    state = fold_induced(
        start_state,
        lax.all_gather(keys, "blk", axis=0, tiled=True),
        lax.all_gather(values, "blk", axis=0, tiled=True),
        lax.all_gather(valid_b, "blk", axis=0, tiled=True),
        inducing,
    )
    induced = state[2] / state[1][..., None]
    induced = jnp.transpose(induced, (1, 0, 2)).reshape(INDUCE, HEADS * HD).astype(jnp.bfloat16)
    rows_f = slate_rows.astype(jnp.float32)
    score, pull = jax.vjp(
        lambda rows: doc_scores(rows, induced, query_weight, out_weight, score_vector), rows_f
    )
    expo = jnp.where(valid, jnp.exp(score), 0.0)
    tag_f = tags.astype(jnp.float32)
    other_tags = lax.all_gather(tag_f, "blk", axis=0, tiled=True)
    other_exp = lax.all_gather(expo, "blk", axis=0, tiled=True)
    keep = other_tags[None, :] >= tag_f[:, None]
    den = jnp.sum(jnp.where(keep, other_exp[None, :], 0.0), axis=1)
    den_safe = jnp.where(valid, den, 1.0)
    loss_rows = jnp.where(valid, jnp.log(den_safe) - score, 0.0)
    slate_loss = lax.psum(jnp.sum(loss_rows), "blk")
    inverse = jnp.where(valid, 1.0 / den_safe, 0.0)
    other_tags = lax.all_gather(tag_f, "blk", axis=0, tiled=True)
    other_inv = lax.all_gather(inverse, "blk", axis=0, tiled=True)
    keep = other_tags[None, :] <= tag_f[:, None]
    acc_inv = jnp.sum(jnp.where(keep, other_inv[None, :], 0.0), axis=1)
    score_grad = jnp.where(valid, expo * acc_inv - 1.0, 0.0)
    slot_grads = pull(score_grad)[0].astype(jnp.bfloat16)
    returned = lax.all_to_all(
        slot_grads.reshape(nbins, slots, width), "bins", split_axis=0, concat_axis=0, tiled=True
    ).reshape(total_slots, width)
    row_grads = jnp.einsum(
        "sc,sd->cd", placed_b, returned, preferred_element_type=jnp.float32
    ).astype(jnp.bfloat16)
    return (row_grads, jnp.reshape(slate_loss, (1,)))


def solution(mesh):
    placed = (
        P(("groups", "bins", "blk"), None),
        P(),
        P(),
        P(("groups", "bins", "blk"), None),
        P(("groups", "bins", "blk"), None),
        P(("groups", "bins", "blk")),
        P(),
        P(),
        P(),
        P(),
        P(),
        P(),
    )
    return jax.shard_map(
        local,
        mesh=mesh,
        in_specs=placed,
        out_specs=(P(("groups", "bins", "blk"), None), P(("groups", "bins"))),
        check_vma=False,
    )
```

profile of v0, /device:TPU:0, one launch (start us, length us, event | category | flops | bytes accessed | tf_op | source)
XLA Modules:
  0.0 165.4 jit_solution(339078073939606467)
XLA Ops:
  7.3 1.0 convert_reduce_fusion
  8.3 1.0 reduce-window.9
  10.2 0.7 fusion.75
  10.9 2.1 %fusion = f32[1024]{0:T(1024)S(1)} fusion(bf16[1024,1024]{1,0:T(8,128)(2,1)} %param.12), kind=kLoop, calls=%fused_computation.3 | loop fusion | flops 3144704 | bytes 2101248 | tf_op jit(solution)/shard_map/reduce_sum | solution.py:61
  13.0 5.9 %fusion.36 = bf16[256,1024]{1,0:T(8,128)(2,1)S(1)} fusion(bf16[1024,1024]{1,0:T(8,128)(2,1)} %param.12, bf16[1024,1024]{1,0:T(8,128)(2,1)} %param.14, f32[1024]{0:T(1024)S(1)} %copy-done.17, f32[1024]{0:T(1024)S(1)} %add_rsqrt_fusion, f32[256]{0:T(256)S(1)} %convert_element_type.114, s32[256]{0:T(256)S(1)} %get-tuple-element.7, s32[256]{0:T(256)S(1)} %get-tuple-element.6), kind=kOutput, calls=%fused_computation.43 | convolution fusion | flops 2693005312 | bytes 4729856 | tf_op jit(solution)/shard_map/dot_general | solution.py:72
  19.3 23.5 %all_to_all.19 = bf16[4,80,1024]{2,1,0:T(8,128)(2,1)S(1)} all-to-all(bf16[4,80,1024]{2,1,0:T(8,128)(2,1)S(1)} %bitcast.89), channel_id=1, replica_groups=mesh['groups'=2,'bins'=4,'blk'=4] {'bins'}, dimensions={0} | all-to-all | bytes 1310720 | tf_op jit(solution)/shard_map/all_to_all | solution.py:87
  42.9 1.7 %convolution_convert_fusion.5 = bf16[320,1024]{1,0:T(8,128)(2,1)} fusion(bf16[320,1024]{1,0:T(8,128)(2,1)S(1)} %bitcast.90, bf16[1024,1024]{1,0:T(8,128)(2,1)S(1)} %copy-done.15), kind=kOutput, calls=%fused_computation.32 | convolution fusion | flops 671416320 | bytes 3407872 | tf_op jit(solution)/shard_map/dot_general | solution.py:95
  44.7 3.3 %convolution_convert_fusion.4 = bf16[320,1024]{1,0:T(8,128)(2,1)} fusion(bf16[320,1024]{1,0:T(8,128)(2,1)S(1)} %bitcast.91, bf16[1024,1024]{1,0:T(8,128)(2,1)} %param.19), kind=kOutput, calls=%fused_computation.31 | convolution fusion | flops 671416320 | bytes 3407872 | tf_op jit(solution)/shard_map/dot_general | solution.py:96
  48.9 3.2 %all-to-all-start = ((s32[4,1,80]{2,1,0:T(1,128)}), s32[4,1,80]{2,1,0:T(1,128)S(1)}, u32[]{:S(2)}, u32[]{:S(2)}) async-start(s32[4,1,80]{2,1,0:T(1,128)} %all_to_all.12), calls=%async_computation | async-start | bytes 4096 | tf_op jit(solution)/shard_map/all_to_all | solution.py:90
  53.5 4.0 %all-to-all-done = s32[4,1,80]{2,1,0:T(1,128)S(1)} async-done(((s32[4,1,80]{2,1,0:T(1,128)}), s32[4,1,80]{2,1,0:T(1,128)S(1)}, u32[]{:S(2)}, u32[]{:S(2)}) %all-to-all-start) | async-done | bytes 1312 | tf_op jit(solution)/shard_map/all_to_all | solution.py:90
  59.3 6.2 %all-reduce = bf16[1280]{0:T(1024)(128)(2,1)S(1)} all-reduce(bf16[1280]{0:T(1024)(128)(2,1)S(1)} %dynamic-update-slice), channel_id=1, replica_groups=mesh['groups'=2,'bins'=4,'blk'=4] {'blk'}, use_global_device_ids=true, to_apply=%add | all-reduce | flops 1280 | bytes 5120
  65.5 0.8 convolution_convert_fusion.3
  66.3 1.2 copy.32
  67.6 2.0 %all-gather.3.cloned.1.call-done = bf16[1280,1024]{1,0:T(8,128)(2,1)} async-done(((bf16[320,1024]{1,0:T(8,128)(2,1)}), bf16[1280,1024]{1,0:T(8,128)(2,1)}) %all-gather.3.cloned.1.call-update) | async-done | bytes 2621456 | tf_op jit(solution)/shard_map/all_gather | solution.py:106
  69.6 4.4 %copy.29 = bf16[1280,1024]{0,1:T(8,128)(2,1)} copy(bf16[1280,1024]{1,0:T(8,128)(2,1)} %all-gather.3.cloned.1.call-done) | data formatting | bytes 5242880 | tf_op jit(solution)/shard_map/all_gather | solution.py:106
  74.0 2.4 %fusion.76 = (f32[16,32]{1,0:T(8,128)S(1)}, f32[16,32,1280]{2,1,0:T(8,128)S(1)}) fusion(bf16[1280,16,64]{0,2,1:T(8,128)(2,1)} %bitcast.84, bf16[32,16,64]{2,1,0:T(8,128)(2,1)S(1)} %reshape.151, pred[1280]{0:T(1024)(128)(4,1)S(1)} %broadcast_compare_fusion), kind=kOutput, calls=%fused_computation.103 | convolution fusion | flops 85851648 | bytes 5311744 | tf_op jit(solution)/shard_map/ihd,nhd->hin/dot_general | solution.py:17
  76.4 1.5 copy-done.1
  78.5 18.2 %all-gather.5.cloned.1.call-done = bf16[1280,1024]{1,0:T(8,128)(2,1)} async-done(((bf16[320,1024]{1,0:T(8,128)(2,1)}), bf16[1280,1024]{1,0:T(8,128)(2,1)}) %all-gather.5.cloned.1.call-update) | async-done | bytes 2621456 | tf_op jit(solution)/shard_map/all_gather | solution.py:107
  96.7 4.4 %copy.31 = bf16[1280,1024]{0,1:T(8,128)(2,1)} copy(bf16[1280,1024]{1,0:T(8,128)(2,1)} %all-gather.5.cloned.1.call-done) | data formatting | bytes 5242880 | tf_op jit(solution)/shard_map/all_gather | solution.py:107
  101.1 3.5 %fusion.43 = bf16[32,16,64]{2,0,1:T(8,128)(2,1)S(1)} fusion(bf16[1280,16,64]{0,2,1:T(8,128)(2,1)} %bitcast.87, f32[16,32,1280]{2,1,0:T(8,128)} %copy-done.1, f32[16,32]{1,0:T(8,128)S(1)} %broadcast_maximum_fusion, pred[1280]{0:T(1024)(128)(4,1)S(1)} %broadcast_compare_fusion, f32[32,16]{0,1:T(8,128)S(1)} %bitcast.102), kind=kOutput, calls=%fused_computation.46 | convolution fusion | flops 85262336 | bytes 5313792 | tf_op jit(solution)/shard_map/hin,nhd->hid/dot_general | solution.py:25
  106.6 1.0 fusion.29
  107.6 0.7 fusion.71
  108.3 10.3 %all-reduce.5 = (f32[1280]{0:T(1024)S(1)}, f32[1280]{0:T(1024)S(1)}) all-reduce(f32[1280]{0:T(1024)S(1)} %fusion.71, f32[1280]{0:T(1024)S(1)} %dynamic-update-slice.1), channel_id=1, replica_groups=mesh['groups'=2,'bins'=4,'blk'=4] {'blk'}, use_global_device_ids=true, to_apply=%add.2 | all-reduce | flops 2560 | bytes 20480
  119.1 0.7 fusion.70
  119.8 1.3 select_reduce_fusion.3
  121.1 6.5 %all-reduce.4 = (f32[1280]{0:T(1024)S(1)}, f32[1]{0:T(128)}) all-reduce(f32[1280]{0:T(1024)S(1)} %fusion.70, f32[1]{0:T(128)} %bitcast.27), channel_id=1, replica_groups=mesh['groups'=2,'bins'=4,'blk'=4] {'blk'}, use_global_device_ids=true, to_apply=%add.3 | all-reduce | flops 1281 | bytes 10248
  128.5 2.5 %fusion.17 = bf16[320,1024]{1,0:T(8,128)(2,1)S(1)} fusion(bf16[1024,1024]{1,0:T(8,128)(2,1)} %param.21, f32[320]{0:T(512)S(1)} %add_select_fusion, f32[1024]{0:T(1024)} %param.23), kind=kOutput, calls=%fused_computation.26 | convolution fusion | flops 671744000 | bytes 2757888 | tf_op jit(solution)/shard_map/transpose(jvp())/dot_general | solution.py:41
  131.0 1.2 copy.33
  132.2 1.5 fusion.49
  134.4 1.1 fusion.21
  135.5 21.8 %all_to_all.20 = bf16[4,80,1024]{2,1,0:T(8,128)(2,1)S(1)} all-to-all(bf16[4,80,1024]{2,1,0:T(8,128)(2,1)S(1)} %bitcast.94), channel_id=1, replica_groups=mesh['groups'=2,'bins'=4,'blk'=4] {'bins'}, dimensions={0} | all-to-all | bytes 1310720 | tf_op jit(solution)/shard_map/all_to_all | solution.py:133
  157.3 1.3 convolution_convert_fusion.7
  (81 shorter events, 9.3 us)
Async XLA Ops:
  7.2 58.3 %copy-start = (bf16[1024,1024]{1,0:T(8,128)(2,1)S(1)}, bf16[1024,1024]{1,0:T(8,128)(2,1)}, u32[]{:S(2)}) copy-start(bf16[1024,1024]{1,0:T(8,128)(2,1)} %param.20) | copy-start | bytes 6291460
  7.2 5.8 %copy-start.12 = (s32[256,1]{0,1:T(1,128)S(1)}, s32[256,1]{0,1:T(1,128)}, u32[]{:S(2)}) copy-start(s32[256,1]{0,1:T(1,128)} %param.16) | copy-start | bytes 3076
  7.2 5.8 %copy-start.14 = (s32[256]{0:T(256)S(1)}, s32[256]{0:T(256)}, u32[]{:S(2)}) copy-start(s32[256]{0:T(256)} %param.17) | copy-start | bytes 3076
  7.2 5.8 %copy-start.17 = (f32[1024]{0:T(1024)S(1)}, f32[1024]{0:T(1024)}, u32[]{:S(2)}) copy-start(f32[1024]{0:T(1024)} %param.13) | copy-start | bytes 12292
  7.2 62.4 %all-gather.3.cloned.1.call-start = ((), (), s32[]{:S(2)}) async-start(), calls=%async_computation.3 | async-start | bytes 3276800 | tf_op jit(solution)/shard_map/all_gather | solution.py:106
  13.0 35.0 %copy-start.10 = (s32[256]{0:T(256)}, s32[256]{0:T(256)S(1)}, u32[]{:S(2)}) copy-start(s32[256]{0:T(256)S(1)} %get-tuple-element.16) | copy-start | bytes 3076
  19.0 23.9 %copy-start.15 = (bf16[1024,1024]{1,0:T(8,128)(2,1)S(1)}, bf16[1024,1024]{1,0:T(8,128)(2,1)}, u32[]{:S(2)}) copy-start(bf16[1024,1024]{1,0:T(8,128)(2,1)} %param.18) | copy-start | bytes 6291460
  44.6 7.5 %copy-start.9 = (bf16[32,1024]{1,0:T(8,128)(2,1)S(1)}, bf16[32,1024]{1,0:T(8,128)(2,1)}, u32[]{:S(2)}) copy-start(bf16[32,1024]{1,0:T(8,128)(2,1)} %param.22) | copy-start | bytes 196612
  44.6 7.7 %copy-start.20 = (u32[32]{0:T(128)S(1)}, u32[32]{0:T(128)}, u32[]{:S(2)}) copy-start(u32[32]{0:T(128)} %constant.40) | copy-start | bytes 388
  44.6 52.1 %all-gather.5.cloned.1.call-start = ((), (), s32[]{:S(2)}) async-start(), calls=%async_computation.4 | async-start | bytes 3276800 | tf_op jit(solution)/shard_map/all_gather | solution.py:107
  48.9 8.7 %all-to-all-start = ((s32[4,1,80]{2,1,0:T(1,128)}), s32[4,1,80]{2,1,0:T(1,128)S(1)}, u32[]{:S(2)}, u32[]{:S(2)}) async-start(s32[4,1,80]{2,1,0:T(1,128)} %all_to_all.12), calls=%async_computation | async-start | bytes 4096 | tf_op jit(solution)/shard_map/all_to_all | solution.py:90
  58.2 0.5 copy-start.13
  76.4 1.5 copy-start.1
  101.1 3.5 %copy-start.2 = (bf16[320,1024]{0,1:T(8,128)(2,1)S(1)}, bf16[320,1024]{0,1:T(8,128)(2,1)}, u32[]{:S(2)}) copy-start(bf16[320,1024]{0,1:T(8,128)(2,1)} %copy.32) | copy-start | bytes 1966084
  104.6 0.9 copy-start.3
  104.9 1.3 copy-start.5
  104.9 1.6 copy-start.16
  105.0 1.6 copy-start.18
  105.1 1.1 copy-start.7
  132.2 1.5 copy-start.4
  132.2 1.6 copy-start.6
  132.2 1.6 copy-start.8
  133.7 0.7 copy-start.19
  134.4 22.9 %copy-start.11 = (s32[256]{0:T(256)S(1)}, s32[256]{0:T(256)}, u32[]{:S(2)}) copy-start(s32[256]{0:T(256)} %copy-done.10) | copy-start | bytes 3076
Sparse Core Ops, SparseCore 0:
  44.7 24.7 all-gather.2
  71.1 25.5 all-gather.4
where the time goes:
time: 166 us; the launch traced here: 165 us
  blocking collectives  68.3 us (41%)
  matrix products  26.5 us (16%)
  waiting for transfers between devices  24.3 us (15%)
  local copies, waits for them, and re-layouts  16.3 us (10%)
  between operations  15.1 us (9%)
  other arithmetic  11.6 us (7%)
  starting transfers between devices  3.3 us (2%)
    all_to_all x1, blocking collectives, local(): lax.all_to_all(send_rows.reshape(nbins, slots, width), 'bins', split_axis...  23.5 us
    unnamed x3, blocking collectives  23 us
    all_to_all x1, blocking collectives, local(): lax.all_to_all(slot_grads.reshape(nbins, slots, width), 'bins', split_axi...  21.8 us
    all_gather x1, waiting for transfers between devices, local(): lax.all_gather(values, 'blk', axis=0, tiled=True)  18.2 us
    dot_general x1, matrix products, local(): jnp.dot(member_tok.astype(jnp.bfloat16), enc_tok, preferred_element_type=...  5.92 us
    all_gather x1, local copies, waits for them, and re-layouts, local(): lax.all_gather(values, 'blk', axis=0, tiled=True)  4.39 us
    all_gather x1, local copies, waits for them, and re-layouts, local(): lax.all_gather(keys, 'blk', axis=0, tiled=True)  4.39 us
    all_to_all x1, waiting for transfers between devices, local(): lax.all_to_all(send_tags.reshape(nbins, slots), 'bins', split_axis=0, con...  4.02 us
  transfers between devices with their start and end apart: 3, of which 3 were waited for; matrix products, arithmetic and copies ran while one was open for 9% of the time, Pallas kernels for 0%

commit v1 on v0

--- a/solution.py
+++ b/solution.py
@@ -1,6 +1,10 @@
+import functools
+
 import jax
 import jax.numpy as jnp
 from jax import lax
+from jax.experimental import pallas as pl
+from jax.experimental.pallas import tpu as pltpu
 from jax.sharding import PartitionSpec as P
 
 HEADS = 16
@@ -139,6 +143,506 @@
     return (row_grads, jnp.reshape(slate_loss, (1,)))
 
 
+MESH = pl.DeviceIdType.MESH
+F32 = jnp.float32
+BF16 = jnp.bfloat16
+NEG = -1e30
+NT = (((1,), (1,)), ((), ()))
+TN = (((0,), (0,)), ((), ()))
+
+
+def dg(a, b, dims):
+    return lax.dot_general(a, b, dims, preferred_element_type=F32)
+
+
+def iota(shape, axis):
+    return lax.broadcasted_iota(jnp.int32, shape, axis)
+
+
+def fused_kernel(
+    tok_hbm, we_hbm, wk_hbm, wv_hbm, wq_hbm, wo_hbm,
+    gain_ref, lens_ref, mem_ref, keys_ref, ind_ref, sv_ref,
+    out_ref, loss_ref,
+    tok, we, wk, wv, wq, wo, etok, pool, enc, kk, vv, qq, bias,
+    sbuf, s1recv, msg, recv2, gath, ubc, prob, srow, dq, bb,
+    comp_all, sc_all,
+    ld_sem, cs_sem, cr_sem, ss_sem, sr_sem, s1s, s1r, s2s, s2r, ags, agr, fws, fwr,
+):
+    nb, nk = 4, 4
+    n = nb * nk
+    width = tok.shape[1]
+    cand = mem_ref.shape[0]
+    ntok = tok.shape[0]
+    total = n * cand
+    hi_rows = nb * total // 128
+    chips = n // 2
+    pairs = HEADS // 2
+    tile = 256
+    mybin, myblk = lax.axis_index("bins"), lax.axis_index("blk")
+    me = mybin * nk + myblk
+    core = lax.rem(myblk, 2)
+    chip = me // 2
+
+    def peer(rank):
+        return {"bins": rank // nk, "blk": lax.rem(rank, nk)}
+
+    sibling = peer(chip * 2 + 1 - core)
+
+    barrier = pltpu.get_barrier_semaphore()
+    for k in range(1, n):
+        pl.semaphore_signal(barrier, inc=1, device_id=peer(lax.rem(me + k, n)), device_id_type=MESH)
+
+    tchunks = ntok // tile
+    loads = [pltpu.make_async_copy(we_hbm, we, ld_sem.at[0])]
+    for k in range(tchunks):
+        loads.append(
+            pltpu.make_async_copy(
+                tok_hbm.at[pl.ds(k * tile, tile)], tok.at[pl.ds(k * tile, tile)], ld_sem.at[5 + k]
+            )
+        )
+    loads.append(pltpu.make_async_copy(wk_hbm, wk, ld_sem.at[1]))
+    loads.append(pltpu.make_async_copy(wv_hbm, wv, ld_sem.at[2]))
+    loads.append(pltpu.make_async_copy(wq_hbm, wq, ld_sem.at[3]))
+    loads.append(pltpu.make_async_copy(wo_hbm, wo, ld_sem.at[4]))
+    for c in loads:
+        c.start()
+
+    rr, cc = iota((cand, cand), 0), iota((cand, cand), 1)
+    lens_row = lens_ref[...].astype(F32)
+    ends = jnp.sum(jnp.where(cc <= rr, lens_row, 0.0), axis=1, keepdims=True)
+    lens_col = jnp.sum(jnp.where(cc == rr, lens_row, 0.0), axis=1, keepdims=True)
+    starts = ends - lens_col
+    pos = iota((cand, ntok), 1).astype(F32)
+    pool[...] = jnp.where((pos >= starts) & (pos < ends), 1.0, 0.0).astype(BF16)
+    inv_len = lens_col
+    slate_col = mem_ref[...].astype(F32)
+    slate_row = jnp.sum(jnp.where(cc == rr, slate_col, 0.0), axis=0, keepdims=True)
+    key_row = keys_ref[...].astype(F32)
+    key_col = jnp.sum(jnp.where(cc == rr, key_row, 0.0), axis=1, keepdims=True)
+    comp_row = (slate_row * float(total) + key_row).astype(jnp.int32)
+    comp_col = (slate_col * float(total) + key_col).astype(jnp.int32)
+    comp_all[me] = comp_row
+    lane_slate = (iota((cand, 128), 1) // INDUCE).astype(F32)
+    bias[...] = jnp.where(lane_slate == slate_col, 0.0, NEG)
+
+    pl.semaphore_wait(barrier, n - 1)
+    comp_sends = []
+    for k in range(1, n):
+        c = pltpu.make_async_remote_copy(
+            src_ref=comp_all.at[me], dst_ref=comp_all.at[me],
+            send_sem=cs_sem.at[k], recv_sem=cr_sem.at[me],
+            device_id=peer(lax.rem(me + k, n)), device_id_type=MESH,
+        )
+        c.start()
+        comp_sends.append(c)
+
+    loads[0].wait()
+
+    def enc_chunk(k, _):
+        rows = pl.ds(pl.multiple_of(k * tile, tile), tile)
+        pltpu.make_async_copy(tok_hbm.at[rows], tok.at[rows], ld_sem.at[5 + k]).wait()
+        x = tok[rows, :].astype(F32)
+        ms = jnp.mean(x * x, axis=-1, keepdims=True)
+        normed = (x * lax.rsqrt(ms + 1e-06) * gain_ref[...]).astype(BF16)
+        for j in range(width // tile):
+            cols = pl.ds(j * tile, tile)
+            y = tok[rows, cols].astype(F32) + jnp.dot(
+                normed, we[:, cols], preferred_element_type=F32
+            )
+            etok[rows, cols] = y.astype(BF16)
+        return 0
+
+    lax.fori_loop(0, tchunks, enc_chunk, 0)
+
+    def tiles(body):
+        def step(j, _):
+            body(pl.ds(pl.multiple_of(j * tile, tile), tile))
+            return 0
+
+        lax.fori_loop(0, width // tile, step, 0)
+
+    def pool_tile(cols):
+        y = jnp.dot(pool[...], etok[:, cols], preferred_element_type=F32)
+        enc[:, cols] = (y / inv_len).astype(BF16)
+
+    tiles(pool_tile)
+
+    def project(w, dst):
+        def body(cols):
+            dst[:, cols] = jnp.dot(enc[...], w[:, cols], preferred_element_type=F32).astype(BF16)
+
+        tiles(body)
+
+    loads[1 + tchunks].wait()
+    project(wk, kk)
+    loads[2 + tchunks].wait()
+    project(wv, vv)
+
+    row8 = iota((8, 128), 0)
+    half_lane = iota((INDUCE, 128), 1) < HD
+
+    def s1_copy(p):
+        return pltpu.make_async_remote_copy(
+            src_ref=sbuf.at[1 - core, p], dst_ref=s1recv.at[p],
+            send_sem=s1s.at[p], recv_sem=s1r.at[p],
+            device_id=sibling, device_id_type=MESH,
+        )
+
+    def partial_pair(p, _):
+        lanes = pl.ds(pl.multiple_of(p * 128, 128), 128)
+        ind = ind_ref[:, lanes].astype(F32)
+        ia = jnp.where(half_lane, ind, 0.0)
+        ib = jnp.where(half_lane, 0.0, ind)
+        bd = jnp.concatenate([ia] * nb + [ib] * nb, axis=0).astype(BF16)
+        s = dg(kk[:, lanes], bd, NT) * 0.125
+        b = bias[...]
+        s = s + jnp.concatenate([b, b], axis=1)
+        top = jnp.maximum(jnp.max(s, axis=0, keepdims=True), -1e29)
+        thi = top.astype(BF16).astype(F32)
+        top = thi + (top - thi).astype(BF16).astype(F32)
+        pr = jnp.exp(s - top)
+        l = jnp.sum(pr, axis=0, keepdims=True)
+        acc = dg(vv[:, lanes], pr.astype(BF16), TN)
+        for h in range(2):
+            hc = slice(h * 128, (h + 1) * 128)
+            sbuf[h, p, 0:HD] = acc[h * HD:(h + 1) * HD, hc]
+            sbuf[h, p, HD:HD + 8] = jnp.where(
+                row8 == 0, top[:, hc], jnp.where(row8 == 1, l[:, hc], 0.0)
+            )
+        s1_copy(p).start()
+        return 0
+
+    lax.fori_loop(0, pairs, partial_pair, 0)
+
+    row16 = iota((16, 128), 0)
+
+    def s2_copy(k):
+        p = lax.rem(chip + k, chips)
+        return pltpu.make_async_remote_copy(
+            src_ref=msg.at[p], dst_ref=recv2.at[chip],
+            send_sem=s2s.at[p], recv_sem=s2r.at[chip],
+            device_id=peer(p * 2 + core), device_id_type=MESH,
+        )
+
+    def merge_pair(k):
+        p = lax.rem(chip + k, chips)
+        s1_copy(p).wait_recv()
+        m0, m1 = sbuf[core, p, HD:HD + 1], s1recv[p, HD:HD + 1]
+        l0, l1 = sbuf[core, p, HD + 1:HD + 2], s1recv[p, HD + 1:HD + 2]
+        mx = jnp.maximum(m0, m1)
+        f0, f1 = jnp.exp(m0 - mx), jnp.exp(m1 - mx)
+        l = l0 * f0 + l1 * f1
+        msg[p, 0:HD] = (sbuf[core, p, 0:HD] * f0 + s1recv[p, 0:HD] * f1).astype(BF16)
+        mhi = mx.astype(BF16).astype(F32)
+        lhi = l.astype(BF16).astype(F32)
+        st = jnp.where(row16 == 0, mhi, jnp.where(row16 == 1, mx - mhi, 0.0))
+        st = jnp.where(row16 == 2, lhi, jnp.where(row16 == 3, l - lhi, st))
+        msg[p, HD:HD + 16] = st.astype(BF16)
+
+    def merge_send(k, _):
+        merge_pair(k)
+        s2_copy(k).start()
+        return 0
+
+    lax.fori_loop(1, chips, merge_send, 0)
+    merge_pair(0)
+
+    loads[3 + tchunks].wait()
+    project(wq, qq)
+    loads[4 + tchunks].wait()
+
+    def u_tile(j, _):
+        rows = pl.ds(pl.multiple_of(j * 128, 128), 128)
+        a = jnp.zeros((128, 128), F32)
+        for c in range(width // 128):
+            cs = slice(c * 128, (c + 1) * 128)
+            a = a + wo[rows, cs].astype(F32) * sv_ref[:, cs]
+        ubc[rows, :] = jnp.broadcast_to(jnp.sum(a, axis=1, keepdims=True), (128, 128))
+        return 0
+
+    lax.fori_loop(0, width // 128, u_tile, 0)
+    esv = jnp.sum(enc[...].astype(F32) * sv_ref[...], axis=1, keepdims=True)
+    esv_row = jnp.sum(jnp.where(cc == rr, esv, 0.0), axis=0, keepdims=True)
+
+    def s2_wait(k, _):
+        src = lax.rem(chip + k, chips)
+        pltpu.make_async_remote_copy(
+            src_ref=msg.at[src], dst_ref=recv2.at[src],
+            send_sem=s2s.at[src], recv_sem=s2r.at[src],
+            device_id=sibling, device_id_type=MESH,
+        ).wait_recv()
+        return 0
+
+    lax.fori_loop(1, chips, s2_wait, 0)
+    recv2[chip] = msg[chip]
+
+    def stats(i):
+        st = recv2[i, HD:HD + 16].astype(F32)
+        return st[0:1] + st[1:2], st[2:3] + st[3:4]
+
+    ml = [stats(i) for i in range(chips)]
+    mx = functools.reduce(jnp.maximum, [m for m, _ in ml])
+    acc = jnp.zeros((HD, 128), F32)
+    lsum = jnp.zeros((1, 128), F32)
+    for i in range(chips):
+        f = jnp.exp(ml[i][0] - mx)
+        lsum = lsum + ml[i][1] * f
+        acc = acc + recv2[i, 0:HD].astype(F32) * f
+    gath[chip, core] = (acc / lsum).astype(BF16)
+
+    def ag_copy(k):
+        return pltpu.make_async_remote_copy(
+            src_ref=gath.at[chip, core], dst_ref=gath.at[chip, core],
+            send_sem=ags.at[k], recv_sem=agr.at[chip],
+            device_id=peer(lax.rem(chip + k, chips) * 2 + core), device_id_type=MESH,
+        )
+
+    def fw_copy(p):
+        return pltpu.make_async_remote_copy(
+            src_ref=gath.at[p, core], dst_ref=gath.at[p, core],
+            send_sem=fws.at[p], recv_sem=fwr.at[p],
+            device_id=sibling, device_id_type=MESH,
+        )
+
+    for k in range(1, chips):
+        ag_copy(k).start()
+    fw_copy(chip).start()
+
+    def comp_wait(k, _):
+        src = lax.rem(me + k, n)
+        pltpu.make_async_remote_copy(
+            src_ref=comp_all.at[src], dst_ref=comp_all.at[src],
+            send_sem=cs_sem.at[k], recv_sem=cr_sem.at[src],
+            device_id=sibling, device_id_type=MESH,
+        ).wait_recv()
+        return 0
+
+    lax.fori_loop(1, n, comp_wait, 0)
+    hrow = iota((hi_rows, cand), 0)
+    lrow = iota((128, cand), 0)
+
+    def onehots(b):
+        cr = comp_all[b]
+        return (cr // 128) == hrow, jnp.where(lax.rem(cr, 128) == lrow, 1.0, 0.0).astype(BF16)
+
+    def valid_step(b, t):
+        lm, rm = onehots(b)
+        return t + dg(jnp.where(lm, 1.0, 0.0).astype(BF16), rm, NT)
+
+    valid = lax.fori_loop(0, n, valid_step, jnp.zeros((hi_rows, 128), F32))
+
+    def forward_block(k, _):
+        src = lax.rem(chip + k, chips)
+        pltpu.make_async_remote_copy(
+            src_ref=gath.at[src, core], dst_ref=gath.at[src, core],
+            send_sem=ags.at[k], recv_sem=agr.at[src],
+            device_id=sibling, device_id_type=MESH,
+        ).wait_recv()
+        fw_copy(src).start()
+        return 0
+
+    lax.fori_loop(1, chips, forward_block, 0)
+
+    def fw_wait(p, _):
+        pltpu.make_async_remote_copy(
+            src_ref=gath.at[p, 1 - core], dst_ref=gath.at[p, 1 - core],
+            send_sem=fws.at[p], recv_sem=fwr.at[p],
+            device_id=sibling, device_id_type=MESH,
+        ).wait_recv()
+        return 0
+
+    lax.fori_loop(0, chips, fw_wait, 0)
+
+    masks = [slate_row == float(s) for s in range(nb)]
+    half_row = iota((128, 128), 0) < HD
+
+    def block_diag(p):
+        g = jnp.concatenate([gath[p, 0], gath[p, 1]], axis=0).astype(F32)
+        return jnp.concatenate(
+            [jnp.where(half_row, g, 0.0), jnp.where(half_row, 0.0, g)], axis=1
+        ).astype(BF16)
+
+    def pick(z):
+        r = z[0:INDUCE]
+        for s in range(1, nb):
+            r = jnp.where(masks[s], z[s * INDUCE:(s + 1) * INDUCE], r)
+        return r
+
+    def spread(a, b):
+        return jnp.concatenate(
+            [jnp.where(m, a, 0.0) for m in masks] + [jnp.where(m, b, 0.0) for m in masks], axis=0
+        ).astype(BF16)
+
+    def wide(x):
+        return jnp.concatenate([x] * (cand // 128), axis=1)
+
+    def score_pair(p, row):
+        lanes = pl.ds(pl.multiple_of(p * 128, 128), 128)
+        bd = block_diag(p)
+        z = dg(bd, qq[:, lanes], (((0,), (1,)), ((), ())))
+        ws = []
+        for h in range(2):
+            zs = pick(z[h * 128:(h + 1) * 128]) * 0.125
+            e = jnp.exp(zs - jnp.max(zs, axis=0, keepdims=True))
+            w = e / jnp.sum(e, axis=0, keepdims=True)
+            prob[p, h * INDUCE:(h + 1) * INDUCE] = w
+            ws.append(w)
+        mix = jnp.dot(bd, spread(ws[0], ws[1]), preferred_element_type=F32)
+        u = wide(ubc[lanes, :])
+        mu = mix * u
+        sa = jnp.sum(mu[0:HD], axis=0, keepdims=True)
+        sb = jnp.sum(mu[HD:2 * HD], axis=0, keepdims=True)
+        r8 = iota((8, cand), 0)
+        srow[p] = jnp.where(r8 == 0, sa, sb)
+        return row + jnp.sum(mix.astype(BF16).astype(F32) * u, axis=0, keepdims=True)
+
+    score_row = lax.fori_loop(0, pairs, score_pair, esv_row)
+    sc_all[me] = score_row
+    sc_sends = []
+    for k in range(1, n):
+        c = pltpu.make_async_remote_copy(
+            src_ref=sc_all.at[me], dst_ref=sc_all.at[me],
+            send_sem=ss_sem.at[k], recv_sem=sr_sem.at[me],
+            device_id=peer(lax.rem(me + k, n)), device_id_type=MESH,
+        )
+        c.start()
+        sc_sends.append(c)
+
+    def back_pair(p, _):
+        lanes = pl.ds(pl.multiple_of(p * 128, 128), 128)
+        bd = block_diag(p)
+        u = ubc[lanes, :]
+        uh = u.astype(BF16)
+        ul = (u - uh.astype(F32)).astype(BF16)
+        t = wide(dg(bd, uh, TN) + dg(bd, ul, TN))
+        ds = []
+        for h in range(2):
+            ts = pick(t[h * 128:(h + 1) * 128])
+            ds.append(prob[p, h * INDUCE:(h + 1) * INDUCE] * (ts - srow[p, h:h + 1]) * 0.125)
+        dq[lanes, :] = jnp.dot(bd, spread(ds[0], ds[1]), preferred_element_type=F32).astype(BF16)
+        return 0
+
+    lax.fori_loop(0, pairs, back_pair, 0)
+
+    def b_tile(cols):
+        y = jnp.dot(wq[cols, :], dq[...], preferred_element_type=F32)
+        bb[:, cols] = jnp.transpose(y) + sv_ref[:, cols]
+
+    tiles(b_tile)
+
+    def sc_wait(k, _):
+        src = lax.rem(me + k, n)
+        pltpu.make_async_remote_copy(
+            src_ref=sc_all.at[src], dst_ref=sc_all.at[src],
+            send_sem=ss_sem.at[k], recv_sem=sr_sem.at[src],
+            device_id=sibling, device_id_type=MESH,
+        ).wait_recv()
+        return 0
+
+    lax.fori_loop(1, n, sc_wait, 0)
+
+    def place(b, carry):
+        t, ssum = carry
+        lm, rm = onehots(b)
+        sc = sc_all[b]
+        e = jnp.exp(sc)
+        eh = e.astype(BF16).astype(F32)
+        both = jnp.concatenate([jnp.where(lm, eh, 0.0), jnp.where(lm, e - eh, 0.0)], axis=0)
+        y = dg(both.astype(BF16), rm, NT)
+        mine = (comp_all[b] // total) == mybin
+        return t + y[0:hi_rows] + y[hi_rows:], ssum + jnp.where(mine, sc, 0.0)
+
+    table, ssum = lax.fori_loop(
+        0, n, place, (jnp.zeros((hi_rows, 128), F32), jnp.zeros((1, cand), F32))
+    )
+
+    ri, ci = iota((128, 128), 0), iota((128, 128), 1)
+    per = hi_rows // nb
+    same = (ri // per) == (ci // per)
+
+    def hdot(a, b):
+        return jnp.dot(a, b, preferred_element_type=F32, precision=lax.Precision.HIGHEST)
+
+    suf = jnp.where(ri >= ci, 1.0, 0.0)
+    pre = jnp.where(ri <= ci, 1.0, 0.0)
+    later = jnp.where(same & (ci > ri), 1.0, 0.0)
+    earlier = jnp.where(same & (ci < ri), 1.0, 0.0)
+
+    def total_of(x):
+        return jnp.broadcast_to(jnp.sum(x, axis=1, keepdims=True), (hi_rows, 128))
+
+    den = hdot(table, suf) + hdot(later, total_of(table))
+    is_valid = valid > 0.5
+    den = jnp.where(is_valid, den, 1.0)
+    ln = jnp.where(is_valid & ((ri // per) == mybin), jnp.log(den), 0.0)
+    loss_ref[0] = jnp.sum(ln) - jnp.sum(ssum)
+    inv = jnp.where(is_valid, 1.0 / den, 0.0)
+    acc2 = hdot(inv, pre) + hdot(earlier, total_of(inv))
+    lc = jnp.where((comp_col // 128) == iota((cand, hi_rows), 1), 1.0, 0.0)
+    mine = hdot(lc, acc2)
+    mine = jnp.where(lax.rem(comp_col, 128) == iota((cand, 128), 1), mine, 0.0)
+    acc_col = jnp.sum(mine, axis=1, keepdims=True)
+    e_col = jnp.exp(jnp.sum(jnp.where(cc == rr, score_row, 0.0), axis=1, keepdims=True))
+    g = e_col * acc_col - 1.0
+    out_ref[...] = (bb[...] * g).astype(BF16)
+
+    for c in comp_sends + sc_sends:
+        c.wait_send()
+    for p in range(pairs):
+        s1_copy(p).wait_send()
+        fw_copy(p).wait_send()
+    for k in range(1, chips):
+        s2_copy(k).wait_send()
+        ag_copy(k).wait_send()
+
+
+def fused(
+    tokens, enc_gain, enc_weight, lengths, membership, target_keys,
+    key_weight, value_weight, query_weight, out_weight, inducing, score_vector,
+):
+    ntok, width = tokens.shape
+    cand = membership.shape[0]
+    n = 16
+    any_spec = pl.BlockSpec(memory_space=pl.ANY)
+    vm = pl.BlockSpec(memory_space=pltpu.VMEM)
+    dma = pltpu.SemaphoreType.DMA
+    mat = pltpu.VMEM((width, width), BF16)
+    rows = pltpu.VMEM((cand, width), BF16)
+    out, loss = pl.pallas_call(
+        fused_kernel,
+        out_shape=(
+            jax.ShapeDtypeStruct((cand, width), BF16),
+            jax.ShapeDtypeStruct((1,), F32),
+        ),
+        in_specs=[any_spec] * 6 + [vm] * 6,
+        out_specs=(vm, pl.BlockSpec(memory_space=pltpu.SMEM)),
+        scratch_shapes=[
+            pltpu.VMEM((ntok, width), BF16), mat, mat, mat, mat, mat,
+            pltpu.VMEM((ntok, width), BF16), pltpu.VMEM((cand, ntok), BF16),
+            rows, rows, rows, rows, pltpu.VMEM((cand, 128), F32),
+            pltpu.VMEM((2, 8, HD + 8, 128), F32), pltpu.VMEM((8, HD + 8, 128), F32),
+            pltpu.VMEM((8, HD + 16, 128), BF16), pltpu.VMEM((8, HD + 16, 128), BF16),
+            pltpu.VMEM((8, 2, HD, 128), BF16), pltpu.VMEM((width, 128), F32),
+            pltpu.VMEM((8, 2 * INDUCE, cand), F32), pltpu.VMEM((8, 8, cand), F32),
+            pltpu.VMEM((width, cand), BF16), pltpu.VMEM((cand, width), F32),
+            pltpu.VMEM((n, 1, cand), jnp.int32), pltpu.VMEM((n, 1, cand), F32),
+            dma((5 + ntok // 256,)), dma((n,)), dma((n,)), dma((n,)), dma((n,)),
+            dma((8,)), dma((8,)), dma((8,)), dma((8,)), dma((8,)), dma((8,)), dma((8,)), dma((8,)),
+        ],
+        compiler_params=pltpu.CompilerParams(
+            collective_id=0, has_side_effects=True, vmem_limit_bytes=56 * 1024 * 1024
+        ),
+        cost_estimate=pl.CostEstimate(
+            flops=8_000_000_000, bytes_accessed=13_000_000, transcendentals=1_000_000
+        ),
+    )(
+        tokens, enc_weight, key_weight, value_weight, query_weight, out_weight,
+        enc_gain.reshape(1, width), lengths, membership, target_keys.reshape(1, cand),
+        inducing, score_vector.reshape(1, width),
+    )
+    return out, loss
+
+
 def solution(mesh):
     placed = (
         P(("groups", "bins", "blk"), None),
@@ -154,8 +658,9 @@
         P(),
         P(),
     )
+    small = mesh.shape["bins"] == 4 and mesh.shape["blk"] == 4
     return jax.shard_map(
-        local,
+        fused if small else local,
         mesh=mesh,
         in_specs=placed,
         out_specs=(P(("groups", "bins", "blk"), None), P(("groups", "bins"))),

time: 166 us -> 49.7 us (0.30)
  blocking collectives: 68.3 us -> 0 us
  Pallas kernels: 0 us -> 43.1 us
  matrix products: 26.5 us -> 0 us
  waiting for transfers between devices: 24.3 us -> 0 us
  local copies, waits for them, and re-layouts: 16.3 us -> 3.34 us
  between operations: 15.1 us -> 2.34 us
  other arithmetic: 11.6 us -> 0 us
  starting transfers between devices: 3.3 us -> 0 us
    all_to_all x2 -> x0, blocking collectives: 45.4 us -> none  [the longest x1 23.5 us: local(): lax.all_to_all(send_rows.reshape(nbins, slots, width), 'bins', split_axis...]
    pallas_call x0 -> x1, Pallas kernels: none -> 43.1 us  [fused(): pl.pallas_call(fused_kernel, out_shape=(jax.ShapeDtypeStruct((cand, width...]
    dot_general x15 -> x0, matrix products: 26.5 us -> none  [the longest x1 5.92 us: local(): jnp.dot(member_tok.astype(jnp.bfloat16), enc_tok, preferred_element_type=...]
    unnamed x3 -> x0, blocking collectives: 23 us -> none
    all_gather x2 -> x0, waiting for transfers between devices: 20.3 us -> none  [the longest x1 18.2 us: local(): lax.all_gather(values, 'blk', axis=0, tiled=True)]
    all_gather x2 -> x0, local copies, waits for them, and re-layouts: 8.79 us -> none  [the longest x1 4.39 us: local(): lax.all_gather(values, 'blk', axis=0, tiled=True)]
    reduce_sum x8 -> x0, other arithmetic: 5.88 us -> none  [the longest x1 2.07 us: local(): meansq = jnp.mean(xf * xf, axis=-1, keepdims=True)]
    all_to_all x1 -> x0, waiting for transfers between devices: 4.02 us -> none  [local(): lax.all_to_all(send_tags.reshape(nbins, slots), 'bins', split_axis=0, con...]
  transfers between devices with their start and end apart: 3 -> 0, of which waited for: 3 -> 0; matrix products, arithmetic and copies ran while one was open for 9% -> 0% of each run, Pallas kernels for 0% -> 0%
where the time goes in v1:
time: 49.7 us; the launch traced here: 48.8 us
  Pallas kernels  43.1 us (87%)
  local copies, waits for them, and re-layouts  3.34 us (7%)
  between operations  2.34 us (5%)
    pallas_call x1, Pallas kernels, fused(): pl.pallas_call(fused_kernel, out_shape=(jax.ShapeDtypeStruct((cand, width...  43.1 us
    unnamed x2, local copies, waits for them, and re-layouts  3.34 us

profile of v1, /device:TPU:0, one launch (start us, length us, event | category | flops | bytes accessed | tf_op | source)
XLA Modules:
  0.0 48.8 jit_solution(8388428677619497390)
XLA Ops:
  0.6 1.5 %copy.14.mem_ref = s32[256,1]{1,0:T(8,128)} copy(s32[256,1]{0,1:T(1,128)} %param.16) | data formatting | bytes 2048 | tf_op args[4]
  2.1 43.1 %shard_map.131 = (bf16[256,1024]{1,0:T(8,128)(2,1)}, f32[1]{0:T(128)}) custom-call(bf16[1024,1024]{1,0:T(8,128)(2,1)} %tok_hbm.1, bf16[1024,1024]{1,0:T(8,128)(2,1)} %we_hbm.1, bf16[1024,1024]{1,0:T(8,128)(2,1)} %wk_hbm.1, bf16[1024,1024]{1,0:T(8,128)(2,1)} %wv_hbm.1, bf16[1024,1024]{1,0:T(8,128)(2,1)} %wq_hbm.1, bf16[1024,1024]{1,0:T(8,128)(2,1)} %wo_hbm.1, ...), custom_call_target="tpu_custom_call" | custom-call | flops 8000000000 | bytes 13000000 | tf_op jit(solution)/shard_map/pallas_call | solution.py:611
  45.2 1.9 %copy.17 = bf16[256,1024]{1,0:T(8,128)(2,1)} copy(bf16[256,1024]{1,0:T(8,128)(2,1)} %get-tuple-element.4) | data formatting | bytes 1048576

commit v2 on v1

--- a/solution.py
+++ b/solution.py
@@ -69,7 +69,8 @@
     )
     lens = lengths[0]
     cand = lens.shape[0]
-    ends = jnp.cumsum(lens)
+    seq = jnp.arange(cand, dtype=jnp.int32)
+    ends = jnp.sum(jnp.where(seq[None, :] <= seq[:, None], lens[None, :], 0), axis=1)
     starts = ends - lens
     position = jnp.arange(tok_count, dtype=jnp.int32)
     member_tok = (position[None, :] >= starts[:, None]) & (position[None, :] < ends[:, None])
@@ -162,16 +163,17 @@
 def fused_kernel(
     tok_hbm, we_hbm, wk_hbm, wv_hbm, wq_hbm, wo_hbm,
     gain_ref, lens_ref, mem_ref, keys_ref, ind_ref, sv_ref,
-    out_ref, loss_ref,
+    bb_hbm, g_ref, loss_ref,
     tok, we, wk, wv, wq, wo, etok, pool, enc, kk, vv, qq, bias,
     sbuf, s1recv, msg, recv2, gath, ubc, prob, srow, dq, bb,
     comp_all, sc_all,
     ld_sem, cs_sem, cr_sem, ss_sem, sr_sem, s1s, s1r, s2s, s2r, ags, agr, fws, fwr,
+    out_sem, rt,
 ):
     nb, nk = 4, 4
     n = nb * nk
     width = tok.shape[1]
-    cand = mem_ref.shape[0]
+    cand = mem_ref.shape[1]
     ntok = tok.shape[0]
     total = n * cand
     hi_rows = nb * total // 128
@@ -204,7 +206,7 @@
     loads.append(pltpu.make_async_copy(wv_hbm, wv, ld_sem.at[2]))
     loads.append(pltpu.make_async_copy(wq_hbm, wq, ld_sem.at[3]))
     loads.append(pltpu.make_async_copy(wo_hbm, wo, ld_sem.at[4]))
-    for c in loads:
+    for c in loads[: 1 + tchunks]:
         c.start()
 
     rr, cc = iota((cand, cand), 0), iota((cand, cand), 1)
@@ -215,8 +217,8 @@
     pos = iota((cand, ntok), 1).astype(F32)
     pool[...] = jnp.where((pos >= starts) & (pos < ends), 1.0, 0.0).astype(BF16)
     inv_len = lens_col
-    slate_col = mem_ref[...].astype(F32)
-    slate_row = jnp.sum(jnp.where(cc == rr, slate_col, 0.0), axis=0, keepdims=True)
+    slate_row = mem_ref[...].astype(F32)
+    slate_col = jnp.sum(jnp.where(cc == rr, slate_row, 0.0), axis=1, keepdims=True)
     key_row = keys_ref[...].astype(F32)
     key_col = jnp.sum(jnp.where(cc == rr, key_row, 0.0), axis=1, keepdims=True)
     comp_row = (slate_row * float(total) + key_row).astype(jnp.int32)
@@ -237,6 +239,8 @@
         comp_sends.append(c)
 
     loads[0].wait()
+    loads[1 + tchunks].start()
+    loads[2 + tchunks].start()
 
     def enc_chunk(k, _):
         rows = pl.ds(pl.multiple_of(k * tile, tile), tile)
@@ -253,6 +257,8 @@
         return 0
 
     lax.fori_loop(0, tchunks, enc_chunk, 0)
+    loads[3 + tchunks].start()
+    loads[4 + tchunks].start()
 
     def tiles(body):
         def step(j, _):
@@ -288,8 +294,8 @@
             device_id=sibling, device_id_type=MESH,
         )
 
-    def partial_pair(p, _):
-        lanes = pl.ds(pl.multiple_of(p * 128, 128), 128)
+    def partial_pair(p):
+        lanes = pl.ds(p * 128, 128)
         ind = ind_ref[:, lanes].astype(F32)
         ia = jnp.where(half_lane, ind, 0.0)
         ib = jnp.where(half_lane, 0.0, ind)
@@ -309,10 +315,13 @@
             sbuf[h, p, HD:HD + 8] = jnp.where(
                 row8 == 0, top[:, hc], jnp.where(row8 == 1, l[:, hc], 0.0)
             )
-        s1_copy(p).start()
-        return 0
-
-    lax.fori_loop(0, pairs, partial_pair, 0)
+
+    for half in range(2):
+        own = range(half * pairs // 2, (half + 1) * pairs // 2)
+        for p in own:
+            partial_pair(p)
+        for p in own:
+            s1_copy(p).start()
 
     row16 = iota((16, 128), 0)
 
@@ -421,13 +430,11 @@
     hrow = iota((hi_rows, cand), 0)
     lrow = iota((128, cand), 0)
 
-    def onehots(b):
+    def valid_step(b, t):
         cr = comp_all[b]
-        return (cr // 128) == hrow, jnp.where(lax.rem(cr, 128) == lrow, 1.0, 0.0).astype(BF16)
-
-    def valid_step(b, t):
-        lm, rm = onehots(b)
-        return t + dg(jnp.where(lm, 1.0, 0.0).astype(BF16), rm, NT)
+        rm = jnp.where(lax.rem(cr, 128) == lrow, 1.0, 0.0).astype(BF16)
+        rt[b] = rm
+        return t + dg(jnp.where((cr // 128) == hrow, 1.0, 0.0).astype(BF16), rm, NT)
 
     valid = lax.fori_loop(0, n, valid_step, jnp.zeros((hi_rows, 128), F32))
 
@@ -477,7 +484,7 @@
         return jnp.concatenate([x] * (cand // 128), axis=1)
 
     def score_pair(p, row):
-        lanes = pl.ds(pl.multiple_of(p * 128, 128), 128)
+        lanes = pl.ds(p * 128, 128)
         bd = block_diag(p)
         z = dg(bd, qq[:, lanes], (((0,), (1,)), ((), ())))
         ws = []
@@ -496,7 +503,9 @@
         srow[p] = jnp.where(r8 == 0, sa, sb)
         return row + jnp.sum(mix.astype(BF16).astype(F32) * u, axis=0, keepdims=True)
 
-    score_row = lax.fori_loop(0, pairs, score_pair, esv_row)
+    score_row = esv_row
+    for p in range(pairs):
+        score_row = score_pair(p, score_row)
     sc_all[me] = score_row
     sc_sends = []
     for k in range(1, n):
@@ -508,8 +517,8 @@
         c.start()
         sc_sends.append(c)
 
-    def back_pair(p, _):
-        lanes = pl.ds(pl.multiple_of(p * 128, 128), 128)
+    def back_pair(p):
+        lanes = pl.ds(p * 128, 128)
         bd = block_diag(p)
         u = ubc[lanes, :]
         uh = u.astype(BF16)
@@ -520,15 +529,17 @@
             ts = pick(t[h * 128:(h + 1) * 128])
             ds.append(prob[p, h * INDUCE:(h + 1) * INDUCE] * (ts - srow[p, h:h + 1]) * 0.125)
         dq[lanes, :] = jnp.dot(bd, spread(ds[0], ds[1]), preferred_element_type=F32).astype(BF16)
-        return 0
-
-    lax.fori_loop(0, pairs, back_pair, 0)
+
+    for p in range(pairs):
+        back_pair(p)
 
     def b_tile(cols):
         y = jnp.dot(wq[cols, :], dq[...], preferred_element_type=F32)
         bb[:, cols] = jnp.transpose(y) + sv_ref[:, cols]
 
     tiles(b_tile)
+    bb_out = pltpu.make_async_copy(bb, bb_hbm, out_sem)
+    bb_out.start()
 
     def sc_wait(k, _):
         src = lax.rem(me + k, n)
@@ -541,50 +552,58 @@
 
     lax.fori_loop(1, n, sc_wait, 0)
 
-    def place(b, carry):
-        t, ssum = carry
-        lm, rm = onehots(b)
-        sc = sc_all[b]
+    per = hi_rows // nb
+    prow = iota((per, cand), 0)
+    spots = jnp.zeros((2 * per, 128), F32)
+    ssum = jnp.zeros((1, cand), F32)
+    for b in range(n):
+        cr, sc = comp_all[b], sc_all[b]
         e = jnp.exp(sc)
         eh = e.astype(BF16).astype(F32)
-        both = jnp.concatenate([jnp.where(lm, eh, 0.0), jnp.where(lm, e - eh, 0.0)], axis=0)
-        y = dg(both.astype(BF16), rm, NT)
-        mine = (comp_all[b] // total) == mybin
-        return t + y[0:hi_rows] + y[hi_rows:], ssum + jnp.where(mine, sc, 0.0)
-
-    table, ssum = lax.fori_loop(
-        0, n, place, (jnp.zeros((hi_rows, 128), F32), jnp.zeros((1, cand), F32))
-    )
+        at = lax.rem(cr, total) // 128 == prow
+        both = jnp.concatenate([jnp.where(at, eh, 0.0), jnp.where(at, e - eh, 0.0)], axis=0)
+        spots = spots + dg(both.astype(BF16), rt[b], NT)
+        ssum = ssum + jnp.where((cr // total) == mybin, sc, 0.0)
+    is_valid = valid > 0.5
+    table = jnp.where(is_valid, jnp.concatenate([spots[0:per] + spots[per:]] * nb, axis=0), 0.0)
 
     ri, ci = iota((128, 128), 0), iota((128, 128), 1)
-    per = hi_rows // nb
     same = (ri // per) == (ci // per)
 
-    def hdot(a, b):
-        return jnp.dot(a, b, preferred_element_type=F32, precision=lax.Precision.HIGHEST)
-
-    suf = jnp.where(ri >= ci, 1.0, 0.0)
-    pre = jnp.where(ri <= ci, 1.0, 0.0)
-    later = jnp.where(same & (ci > ri), 1.0, 0.0)
-    earlier = jnp.where(same & (ci < ri), 1.0, 0.0)
-
-    def total_of(x):
-        return jnp.broadcast_to(jnp.sum(x, axis=1, keepdims=True), (hi_rows, 128))
-
-    den = hdot(table, suf) + hdot(later, total_of(table))
-    is_valid = valid > 0.5
+    def ones_where(m):
+        return jnp.where(m, 1.0, 0.0).astype(BF16)
+
+    def split(x, axis):
+        hi = x.astype(BF16)
+        return jnp.concatenate([hi, (x - hi.astype(F32)).astype(BF16)], axis=axis)
+
+    def scan_keys(x, within, across):
+        y = jnp.dot(split(x, 0), within, preferred_element_type=F32)
+        y = y[0:hi_rows] + y[hi_rows:]
+        z = jnp.dot(across, split(y[:, 128:], 1), preferred_element_type=F32)
+        return y[:, 0:128] + z[:, 0:128] + z[:, 128:]
+
+    all_ones = jnp.ones((128, 128), BF16)
+    suf = jnp.concatenate([ones_where(ri >= ci), all_ones], axis=1)
+    pre = jnp.concatenate([ones_where(ri <= ci), all_ones], axis=1)
+    later = ones_where(same & (ci > ri))
+    earlier = ones_where(same & (ci < ri))
+
+    den = scan_keys(table, suf, later)
     den = jnp.where(is_valid, den, 1.0)
     ln = jnp.where(is_valid & ((ri // per) == mybin), jnp.log(den), 0.0)
     loss_ref[0] = jnp.sum(ln) - jnp.sum(ssum)
     inv = jnp.where(is_valid, 1.0 / den, 0.0)
-    acc2 = hdot(inv, pre) + hdot(earlier, total_of(inv))
-    lc = jnp.where((comp_col // 128) == iota((cand, hi_rows), 1), 1.0, 0.0)
-    mine = hdot(lc, acc2)
+    acc2 = scan_keys(inv, pre, earlier)
+    lc = ones_where((comp_col // 128) == iota((cand, hi_rows), 1))
+    mine = jnp.dot(lc, split(acc2, 1), preferred_element_type=F32)
+    mine = mine[:, 0:128] + mine[:, 128:]
     mine = jnp.where(lax.rem(comp_col, 128) == iota((cand, 128), 1), mine, 0.0)
     acc_col = jnp.sum(mine, axis=1, keepdims=True)
     e_col = jnp.exp(jnp.sum(jnp.where(cc == rr, score_row, 0.0), axis=1, keepdims=True))
     g = e_col * acc_col - 1.0
-    out_ref[...] = (bb[...] * g).astype(BF16)
+    g_ref[...] = jnp.broadcast_to(g, (cand, 128))
+    bb_out.wait()
 
     for c in comp_sends + sc_sends:
         c.wait_send()
@@ -608,14 +627,15 @@
     dma = pltpu.SemaphoreType.DMA
     mat = pltpu.VMEM((width, width), BF16)
     rows = pltpu.VMEM((cand, width), BF16)
-    out, loss = pl.pallas_call(
+    back, grad, loss = pl.pallas_call(
         fused_kernel,
         out_shape=(
-            jax.ShapeDtypeStruct((cand, width), BF16),
+            jax.ShapeDtypeStruct((cand, width), F32),
+            jax.ShapeDtypeStruct((cand, 128), F32),
             jax.ShapeDtypeStruct((1,), F32),
         ),
         in_specs=[any_spec] * 6 + [vm] * 6,
-        out_specs=(vm, pl.BlockSpec(memory_space=pltpu.SMEM)),
+        out_specs=(any_spec, vm, pl.BlockSpec(memory_space=pltpu.SMEM)),
         scratch_shapes=[
             pltpu.VMEM((ntok, width), BF16), mat, mat, mat, mat, mat,
             pltpu.VMEM((ntok, width), BF16), pltpu.VMEM((cand, ntok), BF16),
@@ -628,6 +648,7 @@
             pltpu.VMEM((n, 1, cand), jnp.int32), pltpu.VMEM((n, 1, cand), F32),
             dma((5 + ntok // 256,)), dma((n,)), dma((n,)), dma((n,)), dma((n,)),
             dma((8,)), dma((8,)), dma((8,)), dma((8,)), dma((8,)), dma((8,)), dma((8,)), dma((8,)),
+            dma, pltpu.VMEM((n, 128, cand), BF16),
         ],
         compiler_params=pltpu.CompilerParams(
             collective_id=0, has_side_effects=True, vmem_limit_bytes=56 * 1024 * 1024
@@ -637,10 +658,10 @@
         ),
     )(
         tokens, enc_weight, key_weight, value_weight, query_weight, out_weight,
-        enc_gain.reshape(1, width), lengths, membership, target_keys.reshape(1, cand),
+        enc_gain.reshape(1, width), lengths, membership.reshape(1, cand), target_keys.reshape(1, cand),
         inducing, score_vector.reshape(1, width),
     )
-    return out, loss
+    return (back * grad[:, :1]).astype(BF16), loss
 
 
 def solution(mesh):

time: 49.7 us -> 44.2 us (0.89)
  Pallas kernels: 43.1 us -> 38.1 us
  local copies, waits for them, and re-layouts: 3.34 us -> 1.01 us
  other arithmetic: 0 us -> 2.15 us
    pallas_call x1, Pallas kernels: 43.1 us -> 38.1 us  [fused(): pl.pallas_call(fused_kernel, out_shape=(jax.ShapeDtypeStruct((cand, width...]
    unnamed x2 -> x0, local copies, waits for them, and re-layouts: 3.34 us -> none
    convert_element_type x0 -> x1, other arithmetic: none -> 2.15 us  [fused(): return ((back * grad[:, :1]).astype(BF16), loss)]
    slice x0 -> x1, local copies, waits for them, and re-layouts: none -> 1.01 us  [fused(): return ((back * grad[:, :1]).astype(BF16), loss)]
where the time goes in v2:
time: 44.2 us; the launch traced here: 43.6 us
  Pallas kernels  38.1 us (86%)
  between operations  2.4 us (5%)
  other arithmetic  2.15 us (5%)
  local copies, waits for them, and re-layouts  1.01 us (2%)
    pallas_call x1, Pallas kernels, fused(): pl.pallas_call(fused_kernel, out_shape=(jax.ShapeDtypeStruct((cand, width...  38.1 us
    convert_element_type x1, other arithmetic, fused(): return ((back * grad[:, :1]).astype(BF16), loss)  2.15 us
    slice x1, local copies, waits for them, and re-layouts, fused(): return ((back * grad[:, :1]).astype(BF16), loss)  1.01 us

profile of v2, /device:TPU:0, one launch (start us, length us, event | category | flops | bytes accessed | tf_op | source)
XLA Modules:
  0.0 43.6 jit_solution(5005341817345968736)
XLA Ops:
  0.6 38.1 %shard_map.131 = (f32[256,1024]{1,0:T(8,128)}, f32[256,128]{1,0:T(8,128)}, f32[1]{0:T(128)}) custom-call(bf16[1024,1024]{1,0:T(8,128)(2,1)} %tok_hbm.1, bf16[1024,1024]{1,0:T(8,128)(2,1)} %we_hbm.1, bf16[1024,1024]{1,0:T(8,128)(2,1)} %wk_hbm.1, bf16[1024,1024]{1,0:T(8,128)(2,1)} %wv_hbm.1, bf16[1024,1024]{1,0:T(8,128)(2,1)} %wq_hbm.1, ...), custom_call_target="tpu_custom_call" | custom-call | flops 8000000000 | bytes 13000000 | tf_op jit(solution)/shard_map/pallas_call | solution.py:630
  38.7 1.0 %slice_reduce_fusion = f32[256]{0:T(256)S(1)} fusion(f32[256,128]{1,0:T(8,128)} %get-tuple-element.6), kind=kLoop, calls=%fused_computation.1 | loop fusion | bytes 2048 | tf_op jit(solution)/shard_map/slice | solution.py:664
  39.7 2.1 %multiply_convert_fusion = bf16[256,1024]{1,0:T(8,128)(2,1)} fusion(f32[256,1024]{1,0:T(8,128)} %get-tuple-element.5, f32[256]{0:T(256)S(1)} %slice_reduce_fusion), kind=kLoop, calls=%fused_computation | loop fusion | flops 524288 | bytes 1573888 | tf_op jit(solution)/shard_map/convert_element_type | solution.py:664

commit v3 on v2

--- a/solution.py
+++ b/solution.py
@@ -163,12 +163,12 @@
 def fused_kernel(
     tok_hbm, we_hbm, wk_hbm, wv_hbm, wq_hbm, wo_hbm,
     gain_ref, lens_ref, mem_ref, keys_ref, ind_ref, sv_ref,
-    bb_hbm, g_ref, loss_ref,
+    out_ref, loss_ref,
     tok, we, wk, wv, wq, wo, etok, pool, enc, kk, vv, qq, bias,
     sbuf, s1recv, msg, recv2, gath, ubc, prob, srow, dq, bb,
     comp_all, sc_all,
     ld_sem, cs_sem, cr_sem, ss_sem, sr_sem, s1s, s1r, s2s, s2r, ags, agr, fws, fwr,
-    out_sem, rt,
+    rt,
 ):
     nb, nk = 4, 4
     n = nb * nk
@@ -242,9 +242,9 @@
     loads[1 + tchunks].start()
     loads[2 + tchunks].start()
 
-    def enc_chunk(k, _):
-        rows = pl.ds(pl.multiple_of(k * tile, tile), tile)
-        pltpu.make_async_copy(tok_hbm.at[rows], tok.at[rows], ld_sem.at[5 + k]).wait()
+    for k in range(tchunks):
+        rows = pl.ds(k * tile, tile)
+        loads[1 + k].wait()
         x = tok[rows, :].astype(F32)
         ms = jnp.mean(x * x, axis=-1, keepdims=True)
         normed = (x * lax.rsqrt(ms + 1e-06) * gain_ref[...]).astype(BF16)
@@ -254,18 +254,13 @@
                 normed, we[:, cols], preferred_element_type=F32
             )
             etok[rows, cols] = y.astype(BF16)
-        return 0
-
-    lax.fori_loop(0, tchunks, enc_chunk, 0)
+
     loads[3 + tchunks].start()
     loads[4 + tchunks].start()
 
     def tiles(body):
-        def step(j, _):
-            body(pl.ds(pl.multiple_of(j * tile, tile), tile))
-            return 0
-
-        lax.fori_loop(0, width // tile, step, 0)
+        for j in range(width // tile):
+            body(pl.ds(j * tile, tile))
 
     def pool_tile(cols):
         y = jnp.dot(pool[...], etok[:, cols], preferred_element_type=F32)
@@ -538,8 +533,6 @@
         bb[:, cols] = jnp.transpose(y) + sv_ref[:, cols]
 
     tiles(b_tile)
-    bb_out = pltpu.make_async_copy(bb, bb_hbm, out_sem)
-    bb_out.start()
 
     def sc_wait(k, _):
         src = lax.rem(me + k, n)
@@ -602,8 +595,7 @@
     acc_col = jnp.sum(mine, axis=1, keepdims=True)
     e_col = jnp.exp(jnp.sum(jnp.where(cc == rr, score_row, 0.0), axis=1, keepdims=True))
     g = e_col * acc_col - 1.0
-    g_ref[...] = jnp.broadcast_to(g, (cand, 128))
-    bb_out.wait()
+    out_ref[...] = (bb[...] * g).astype(BF16)
 
     for c in comp_sends + sc_sends:
         c.wait_send()
@@ -627,15 +619,14 @@
     dma = pltpu.SemaphoreType.DMA
     mat = pltpu.VMEM((width, width), BF16)
     rows = pltpu.VMEM((cand, width), BF16)
-    back, grad, loss = pl.pallas_call(
+    out, loss = pl.pallas_call(
         fused_kernel,
         out_shape=(
-            jax.ShapeDtypeStruct((cand, width), F32),
-            jax.ShapeDtypeStruct((cand, 128), F32),
+            jax.ShapeDtypeStruct((cand, width), BF16),
             jax.ShapeDtypeStruct((1,), F32),
         ),
         in_specs=[any_spec] * 6 + [vm] * 6,
-        out_specs=(any_spec, vm, pl.BlockSpec(memory_space=pltpu.SMEM)),
+        out_specs=(vm, pl.BlockSpec(memory_space=pltpu.SMEM)),
         scratch_shapes=[
             pltpu.VMEM((ntok, width), BF16), mat, mat, mat, mat, mat,
             pltpu.VMEM((ntok, width), BF16), pltpu.VMEM((cand, ntok), BF16),
@@ -648,7 +639,7 @@
             pltpu.VMEM((n, 1, cand), jnp.int32), pltpu.VMEM((n, 1, cand), F32),
             dma((5 + ntok // 256,)), dma((n,)), dma((n,)), dma((n,)), dma((n,)),
             dma((8,)), dma((8,)), dma((8,)), dma((8,)), dma((8,)), dma((8,)), dma((8,)), dma((8,)),
-            dma, pltpu.VMEM((n, 128, cand), BF16),
+            pltpu.VMEM((n, 128, cand), BF16),
         ],
         compiler_params=pltpu.CompilerParams(
             collective_id=0, has_side_effects=True, vmem_limit_bytes=56 * 1024 * 1024
@@ -661,7 +652,7 @@
         enc_gain.reshape(1, width), lengths, membership.reshape(1, cand), target_keys.reshape(1, cand),
         inducing, score_vector.reshape(1, width),
     )
-    return (back * grad[:, :1]).astype(BF16), loss
+    return out, loss
 
 
 def solution(mesh):

time: 44.2 us -> 40.7 us (0.921)
  other arithmetic: 2.15 us -> 0 us
  Pallas kernels: 38.1 us -> 36.2 us
  local copies, waits for them, and re-layouts: 1.01 us -> 1.87 us
    convert_element_type x1 -> x0, other arithmetic: 2.15 us -> none  [fused(): return ((back * grad[:, :1]).astype(BF16), loss)]
    unnamed x0 -> x1, local copies, waits for them, and re-layouts: none -> 1.87 us
    pallas_call x1, Pallas kernels: 38.1 us -> 36.2 us  [fused(): pl.pallas_call(fused_kernel, out_shape=(jax.ShapeDtypeStruct((cand, width...]
    slice x1 -> x0, local copies, waits for them, and re-layouts: 1.01 us -> none  [fused(): return ((back * grad[:, :1]).astype(BF16), loss)]
where the time goes in v3:
time: 40.7 us; the launch traced here: 40.5 us
  Pallas kernels  36.2 us (89%)
  between operations  2.34 us (6%)
  local copies, waits for them, and re-layouts  1.87 us (5%)
    pallas_call x1, Pallas kernels, fused(): pl.pallas_call(fused_kernel, out_shape=(jax.ShapeDtypeStruct((cand, width...  36.2 us
    unnamed x1, local copies, waits for them, and re-layouts  1.87 us

profile of v3, /device:TPU:0, one launch (start us, length us, event | category | flops | bytes accessed | tf_op | source)
XLA Modules:
  0.0 40.5 jit_solution(8301785443128148203)
XLA Ops:
  0.6 36.2 %shard_map.131 = (bf16[256,1024]{1,0:T(8,128)(2,1)}, f32[1]{0:T(128)}) custom-call(bf16[1024,1024]{1,0:T(8,128)(2,1)} %tok_hbm.1, bf16[1024,1024]{1,0:T(8,128)(2,1)} %we_hbm.1, bf16[1024,1024]{1,0:T(8,128)(2,1)} %wk_hbm.1, bf16[1024,1024]{1,0:T(8,128)(2,1)} %wv_hbm.1, bf16[1024,1024]{1,0:T(8,128)(2,1)} %wq_hbm.1, bf16[1024,1024]{1,0:T(8,128)(2,1)} %wo_hbm.1, ...), custom_call_target="tpu_custom_call" | custom-call | flops 8000000000 | bytes 13000000 | tf_op jit(solution)/shard_map/pallas_call | solution.py:622
  36.9 1.9 %copy.16 = bf16[256,1024]{1,0:T(8,128)(2,1)} copy(bf16[256,1024]{1,0:T(8,128)(2,1)} %get-tuple-element.4) | data formatting | bytes 1048576
